TPU v7x, 32 devices: a whole 2x2x4 slice. The times are simulated.
32 devices in a mesh: dp: 16 (over z, y, x), mp: 2 (over core).
Axes of the slice: x: 2, y: 2, z: 4, core: 2. Of those that a mesh axis runs over, the one named last changes fastest.
Arguments:
- tokens: bfloat16 [1536, 16, 1024], P('mp', 'dp'), may hold values from -6 to 6
- segment_ids: int32 [16, 1536], P('dp'), may hold values from 0 to 1, as said below
- keep_mask: int32 [16, 1536], P('dp'), may hold values from 0 to 1, as said below
- w_query: bfloat16 [1024, 1024], P(None, 'mp'), may hold values from -0.375 to 0.375
- w_key: bfloat16 [1024, 1024], P(None, 'mp'), may hold values from -0.1875 to 0.1875
- w_value: bfloat16 [1024, 1024], P(None, 'mp'), may hold values from -0.1875 to 0.1875
- w_out: bfloat16 [1024, 1024], P('mp'), may hold values from -1 to 1
- w_gate: bfloat16 [1024, 2816], P(None, 'mp'), may hold values from -0.1875 to 0.1875
- w_up: bfloat16 [1024, 2816], P(None, 'mp'), may hold values from -0.1875 to 0.1875
- w_down: bfloat16 [2816, 1024], P('mp'), may hold values from -0.109375 to 0.109375
- norm_attn: float32 [1024], replicated, may hold values from 0.25 to 1.75
- norm_ffn: float32 [1024], replicated, may hold values from 0.25 to 1.75
- cotangent: bfloat16 [1536, 16, 1024], P('mp', 'dp'), may hold values from -6 to 6
Outputs:
- result: bfloat16 [1536, 16, 1024], P('mp', 'dp')
- grad_tokens: bfloat16 [1536, 16, 1024], P('mp', 'dp')
- grad_w_query: float32 [1024, 1024], P(None, 'mp')
- grad_w_key: float32 [1024, 1024], P(None, 'mp')
- grad_w_value: float32 [1024, 1024], P(None, 'mp')
- grad_w_out: float32 [1024, 1024], P('mp')
- grad_w_gate: float32 [1024, 2816], P(None, 'mp')
- grad_w_up: float32 [1024, 2816], P(None, 'mp')
- grad_w_down: float32 [2816, 1024], P('mp')
- grad_norm_attn: float32 [1024], replicated
- grad_norm_ffn: float32 [1024], replicated
Inputs may be any that keep to these rules, and one draw needn't show every extreme that they name: `segment_ids`: each packed row holds one source row of 1152 tokens starting at token 0 or 384; the other 384 tokens are one source row with its own id, or padding that carries the long row's id. `keep_mask`: 0 exactly on the padding described for segment_ids.
All inputs are finite; a program needn't handle non-finite values.
Results may differ from a plain program's by a relative error of at most 0.019.
The roundings to bfloat16 on the way count: a program that leaves them out, or rounds other values in their place, can miss the bound.
Values may be sent and summed in bfloat16 or wider, within the bound.
No kernel may reach another device: no remote copies, remote signals or barrier semaphores. Data moves between devices by JAX's collectives and lax.ppermute only.
A program may use at most 256 MiB of HBM per device.

v0:
```python
import jax
import jax.numpy as jnp
from jax import lax
from jax.sharding import PartitionSpec as P

HDIM = 64


EPSILON = 1e-06
MASKED_SCORE = -1e30


def normalize(value, gain):
    return value * lax.rsqrt(jnp.mean(value * value, axis=-1, keepdims=True) + EPSILON) * gain


def masked_scores(query_block, keys, seg_block, segments, keep_row, heads):
    query_heads = query_block.reshape(query_block.shape[0], heads, -1)
    key_heads = keys.reshape(keys.shape[0], heads, -1)
    scores = jnp.einsum("qhd,khd->hqk", query_heads, key_heads, preferred_element_type=jnp.float32)
    scores = scores * query_heads.shape[-1] ** (-0.5)
    allowed = (seg_block[:, None] == segments[None, :]) & (keep_row[None, :] > 0)
    return jnp.where(allowed[None], scores, MASKED_SCORE)


def attend_row(query, keys, values, segments, keep_row, heads, block_len):
    block_count = query.shape[0] // block_len
    value_heads = values.reshape(values.shape[0], heads, -1)

    def single_block(inputs):
        query_block, seg_block = inputs
        scores = masked_scores(query_block, keys, seg_block, segments, keep_row, heads)
        highest = jnp.max(scores, axis=-1, keepdims=True)
        raised = jnp.exp(scores - highest)
        summed = jnp.sum(raised, axis=-1, keepdims=True)
        probs_low = (raised / summed).astype(jnp.bfloat16)
        mixed = jnp.einsum(
            "hqk,khd->qhd", probs_low, value_heads, preferred_element_type=jnp.float32
        )
        return (
            mixed.reshape(block_len, -1).astype(jnp.bfloat16),
            (highest + jnp.log(summed))[..., 0],
        )

    mixed, log_total = lax.map(
        single_block,
        (query.reshape(block_count, block_len, -1), segments.reshape(block_count, block_len)),
    )
    return (mixed.reshape(query.shape[0], -1), log_total)


def attend_row_back(
    query, keys, values, grad_mixed, log_total, segments, keep_row, heads, block_len
):
    seq_len = query.shape[0]
    inner_width = query.shape[1]
    block_count = seq_len // block_len
    key_heads = keys.reshape(seq_len, heads, -1)
    value_heads = values.reshape(seq_len, heads, -1)
    score_scale = key_heads.shape[-1] ** (-0.5)

    def single_block(accum_pair, inputs):
        query_block, seg_block, grad_block, total_block = inputs
        scores = masked_scores(query_block, keys, seg_block, segments, keep_row, heads)
        probs = jnp.exp(scores - total_block[..., None])
        grad_heads = grad_block.reshape(block_len, heads, -1)
        query_heads = query_block.reshape(block_len, heads, -1)
        dprob = jnp.einsum(
            "qhd,khd->hqk", grad_heads, value_heads, preferred_element_type=jnp.float32
        )
        spread = jnp.sum(dprob * probs, axis=-1, keepdims=True)
        dscore = (probs * (dprob - spread)).astype(jnp.bfloat16)
        grad_query = (
            jnp.einsum("hqk,khd->qhd", dscore, key_heads, preferred_element_type=jnp.float32)
            * score_scale
        )
        grad_key = (
            accum_pair[0]
            + jnp.einsum("hqk,qhd->khd", dscore, query_heads, preferred_element_type=jnp.float32)
            * score_scale
        )
        grad_value = accum_pair[1] + jnp.einsum(
            "hqk,qhd->khd",
            probs.astype(jnp.bfloat16),
            grad_heads,
            preferred_element_type=jnp.float32,
        )
        return ((grad_key, grad_value), grad_query.reshape(block_len, -1).astype(jnp.bfloat16))

    empty_acc = jnp.zeros(key_heads.shape, jnp.float32)
    block_inputs = (
        query.reshape(block_count, block_len, inner_width),
        segments.reshape(block_count, block_len),
        grad_mixed.reshape(block_count, block_len, inner_width),
        log_total,
    )
    (grad_key, grad_value), grad_query = lax.scan(
        single_block, (empty_acc, empty_acc), block_inputs
    )
    return (
        grad_query.reshape(seq_len, inner_width),
        grad_key.reshape(seq_len, inner_width).astype(jnp.bfloat16),
        grad_value.reshape(seq_len, inner_width).astype(jnp.bfloat16),
    )


def activate(gate_proj, up_proj):
    return jax.nn.gelu(gate_proj, approximate=True) * up_proj


def shards(
    tokens,
    segment_ids,
    keep_mask,
    w_query,
    w_key,
    w_value,
    w_out,
    w_gate,
    w_up,
    w_down,
    norm_attn,
    norm_ffn,
    cotangent,
):
    seq_len = segment_ids.shape[1]
    block_len = min(512, seq_len)
    heads = w_query.shape[1] // HDIM
    inner_width = w_query.shape[1]
    ffn_width = w_gate.shape[1]
    residual = tokens.astype(jnp.float32)
    attn_normed, pull_attn = jax.vjp(normalize, residual, norm_attn)
    gathered_attn = lax.all_gather(attn_normed.astype(jnp.bfloat16), "mp", axis=0, tiled=True)
    w_qkv = jnp.concatenate([w_query, w_key, w_value], axis=1)
    projected = jnp.einsum(
        "lrd,de->lre", gathered_attn, w_qkv, preferred_element_type=jnp.float32
    ).astype(jnp.bfloat16)
    rows_first = jnp.moveaxis(projected, 1, 0)
    query = rows_first[..., :inner_width]
    keys = rows_first[..., inner_width : 2 * inner_width]
    values = rows_first[..., 2 * inner_width :]

    def forward_row(inputs):
        return attend_row(inputs[0], inputs[1], inputs[2], inputs[3], inputs[4], heads, block_len)

    mixed_rows, log_totals = lax.map(forward_row, (query, keys, values, segment_ids, keep_mask))
    mixed = jnp.moveaxis(mixed_rows, 0, 1)
    row_piece = mixed
    hidden_state = residual + lax.psum_scatter(
        jnp.einsum("lre,ed->lrd", row_piece, w_out, preferred_element_type=jnp.float32),
        "mp",
        scatter_dimension=0,
        tiled=True,
    )
    ffn_normed, pull_ffn = jax.vjp(normalize, hidden_state, norm_ffn)
    gathered_ffn = lax.all_gather(ffn_normed.astype(jnp.bfloat16), "mp", axis=0, tiled=True)
    w_both = jnp.concatenate([w_gate, w_up], axis=1)
    both_proj = jnp.einsum("lrd,df->lrf", gathered_ffn, w_both, preferred_element_type=jnp.float32)
    activated, pull_act = jax.vjp(activate, both_proj[..., :ffn_width], both_proj[..., ffn_width:])
    activated_low = activated.astype(jnp.bfloat16)
    row_piece = activated_low
    output = hidden_state + lax.psum_scatter(
        jnp.einsum("lrf,fd->lrd", row_piece, w_down, preferred_element_type=jnp.float32).astype(
            jnp.bfloat16
        ),
        "mp",
        scatter_dimension=0,
        tiled=True,
    ).astype(jnp.float32)
    result = output.astype(jnp.bfloat16)
    grad_output = cotangent.astype(jnp.float32)
    grad_down_in = lax.all_gather(cotangent, "mp", axis=0, tiled=True)
    grad_w_down = jnp.einsum(
        "lrf,lrd->fd", activated_low, grad_down_in, preferred_element_type=jnp.float32
    )
    grad_act = jnp.einsum("lrd,fd->lrf", grad_down_in, w_down, preferred_element_type=jnp.float32)
    grad_gate, grad_up = pull_act(grad_act)
    grad_proj = jnp.concatenate([grad_gate, grad_up], axis=-1).astype(jnp.bfloat16)
    grad_w_both = jnp.einsum(
        "lrd,lrf->df", gathered_ffn, grad_proj, preferred_element_type=jnp.float32
    )
    row_piece = grad_proj
    grad_ffn_normed = lax.psum_scatter(
        jnp.einsum("lrf,df->lrd", row_piece, w_both, preferred_element_type=jnp.float32).astype(
            jnp.bfloat16
        ),
        "mp",
        scatter_dimension=0,
        tiled=True,
    ).astype(jnp.float32)
    grad_hidden_norm, gain_ffn_part = pull_ffn(grad_ffn_normed)
    grad_hidden = grad_hidden_norm + grad_output
    grad_w_gate = grad_w_both[:, :ffn_width]
    grad_w_up = grad_w_both[:, ffn_width:]
    grad_attn_in = lax.all_gather(grad_hidden.astype(jnp.bfloat16), "mp", axis=0, tiled=True)
    grad_w_out = jnp.einsum("lre,lrd->ed", mixed, grad_attn_in, preferred_element_type=jnp.float32)
    grad_mixed = jnp.einsum(
        "lrd,ed->lre", grad_attn_in, w_out, preferred_element_type=jnp.float32
    ).astype(jnp.bfloat16)

    def backward_row(inputs):
        return attend_row_back(
            inputs[0],
            inputs[1],
            inputs[2],
            inputs[3],
            inputs[4],
            inputs[5],
            inputs[6],
            heads,
            block_len,
        )

    grad_q_rows, grad_k_rows, grad_v_rows = lax.map(
        backward_row,
        (query, keys, values, jnp.moveaxis(grad_mixed, 1, 0), log_totals, segment_ids, keep_mask),
    )
    grad_qkv = jnp.moveaxis(jnp.concatenate([grad_q_rows, grad_k_rows, grad_v_rows], axis=-1), 0, 1)
    grad_w_qkv = jnp.einsum(
        "lrd,lre->de", gathered_attn, grad_qkv, preferred_element_type=jnp.float32
    )
    row_piece = grad_qkv
    grad_attn_normed = lax.psum_scatter(
        jnp.einsum("lre,de->lrd", row_piece, w_qkv, preferred_element_type=jnp.float32).astype(
            jnp.bfloat16
        ),
        "mp",
        scatter_dimension=0,
        tiled=True,
    ).astype(jnp.float32)
    grad_input_norm, gain_attn_part = pull_attn(grad_attn_normed)
    grad_tokens = (grad_input_norm + grad_hidden).astype(jnp.bfloat16)
    grad_w_query = grad_w_qkv[:, :inner_width]
    grad_w_key = grad_w_qkv[:, inner_width : 2 * inner_width]
    grad_w_value = grad_w_qkv[:, 2 * inner_width :]
    (
        grad_w_query,
        grad_w_key,
        grad_w_value,
        grad_w_out,
        grad_w_gate,
        grad_w_up,
        grad_w_down,
        gain_attn_part,
        gain_ffn_part,
    ) = lax.psum(
        (
            grad_w_query,
            grad_w_key,
            grad_w_value,
            grad_w_out,
            grad_w_gate,
            grad_w_up,
            grad_w_down,
            gain_attn_part,
            gain_ffn_part,
        ),
        "dp",
    )
    grad_norm_attn, grad_norm_ffn = lax.psum((gain_attn_part, gain_ffn_part), "mp")
    return (
        result,
        grad_tokens,
        grad_w_query,
        grad_w_key,
        grad_w_value,
        grad_w_out,
        grad_w_gate,
        grad_w_up,
        grad_w_down,
        grad_norm_attn,
        grad_norm_ffn,
    )


def solution(mesh):
    return jax.shard_map(
        shards,
        mesh=mesh,
        in_specs=(
            P("mp", "dp", None),
            P("dp", None),
            P("dp", None),
            P(None, "mp"),
            P(None, "mp"),
            P(None, "mp"),
            P("mp", None),
            P(None, "mp"),
            P(None, "mp"),
            P("mp", None),
            P(),
            P(),
            P("mp", "dp", None),
        ),
        out_specs=(
            P("mp", "dp", None),
            P("mp", "dp", None),
            P(None, "mp"),
            P(None, "mp"),
            P(None, "mp"),
            P("mp", None),
            P(None, "mp"),
            P(None, "mp"),
            P("mp", None),
            P(),
            P(),
        ),
        check_vma=False,
    )
```

profile of v0, /device:TPU:0, one launch (start us, length us, event | category | flops | bytes accessed | tf_op | source)
XLA Modules:
  0.0 1359.2 jit_solution(2893901180486289349)
XLA Ops:
  19.2 9.2 all-gather.5.cloned.1.call-done
  28.4 7.7 fusion.25
  45.5 116.2 %while.47 = (s32[]{:T(128)}, bf16[3,512,512]{2,1,0:T(8,128)(2,1)}, f32[3,8,512]{2,1,0:T(8,128)S(1)}, s32[3,512]{1,0:T(4,128)S(1)}, s32[1536]{0:T(1024)S(1)}, /*i...) while((s32[]{:T(128)}, bf16[3,512,512]{2,1,0:T(8,128)(2,1)}, ...), condition=%wide.region_4.5_spmd, body=%wide.region_1.4_spmd.sunk | while | flops 1687942656 | bytes 98718888 | solution.py:45
  47.3 10.7 fusion.122
  57.9 11.8 fusion.123
  69.7 12.3 fusion.124
  85.9 10.7 fusion.122
  96.6 11.8 fusion.123
  108.4 12.3 fusion.124
  124.6 10.7 fusion.122
  135.3 11.8 fusion.123
  147.0 12.3 fusion.124
  161.7 6.1 convolution_bitcast_fusion.1
  167.9 15.8 %reduce-scatter.5.cloned.1.call-done = f32[768,1,1024]{2,0,1:T(8,128)} async-done(((f32[1536,1,1024]{2,0,1:T(8,128)}), f32[768,1,1024]{2,0,1:T(8,128)}) %reduce-scatter.5.cloned.1.call-update) | async-done | bytes 3145744 | tf_op jit(solution)/shard_map/reduce_scatter | solution.py:149
  195.8 7.2 all-gather.7.cloned.1.call-done
  203.1 15.8 %convolution_bitcast_fusion = f32[1536,1,2816]{2,0,1:T(8,128)} fusion(bf16[1024,2816]{1,0:T(8,128)(2,1)} %constant_dynamic-update-slice_fusion.5, bf16[1536,1,1024]{2,0,1:T(8,128)(2,1)} %all-gather.7.cloned.1.call-done), kind=kOutput, calls=%fused_computation.34 | convolution fusion | flops 8858370048 | bytes 26214400 | tf_op jit(solution)/shard_map/lrd,df->lrf/dot_general | solution.py:158
  218.8 17.9 %fusion.30 = (bf16[1536,1408]{1,0:T(8,128)(2,1)S(1)}, bf16[1536,1408]{1,0:T(8,128)(2,1)}, bf16[1536,1408]{1,0:T(8,128)(2,1)}) fusion(f32[1536,1,2816]{2,0,1:T(8,128)} %convolution_bitcast_fusion, bf16[1408,1024]{1,0:T(8,128)(2,1)S(1)} %copy-done, bf16[1536,1,1024]{2,0,1:T(8,128)(2,1)} %all-gather.9.cloned.1.call-done), kind=kOutput, calls=%fused_computation.64 | convolution fusion | flops 4485414912 | bytes 36306944 | tf_op jit(solution)/shard_map/lrd,fd->lrf/dot_general | solution.py:176
  238.8 13.8 %fusion.36 = bf16[1536,1,1024]{2,0,1:T(8,128)(2,1)} fusion(bf16[1024,2816]{1,0:T(8,128)(2,1)} %constant_dynamic-update-slice_fusion.5, bf16[1536,1408]{1,0:T(8,128)(2,1)} %get-tuple-element.364, bf16[1536,1408]{1,0:T(8,128)(2,1)S(1)} %get-tuple-element.363), kind=kOutput, calls=%fused_computation.77 | convolution fusion | flops 8877244416 | bytes 17563648 | tf_op jit(solution)/shard_map/lrf,df->lrd/dot_general | solution.py:184
  252.6 11.2 all-gather.11.cloned.1.call-start
  272.6 13.4 all-gather.11.cloned.1.call-done
  292.4 269.2 %while.48 = (s32[]{:T(128)}, f32[1536,8,64]{0,2,1:T(8,128)}, f32[1536,8,64]{0,2,1:T(8,128)}, bf16[3,512,512]{2,1,0:T(8,128)(2,1)}, bf16[3,512,512]{1,2,0:T(8,128...) while((s32[]{:T(128)}, f32[1536,8,64]{0,2,1:T(8,128)}, ...), condition=%wide.region_12.13_spmd.clone, body=%wide.region_10.12_spmd.clone.sunk | while | flops 4089181696 | bytes 219780336 | solution.py:97
  297.5 13.2 subtract_exponential_fusion.3
  310.7 12.1 fusion.136
  322.8 16.5 %multiply_reduce_fusion.3 = (f32[8,512]{1,0:T(8,128)S(1)}, f32[8,512,1536]{2,1,0:T(8,128)}) fusion(f32[8,512,1536]{2,1,0:T(8,128)} %subtract_exponential_fusion.3, bf16[512,8,64]{0,2,1:T(8,128)(2,1)S(1)} %bitcast.169, bf16[1536,8,64]{0,2,1:T(8,128)(2,1)} %get-tuple-element.590), kind=kOutput, calls=%fused_computation.16.clone.1 | convolution fusion | flops 817885184 | bytes 52445184 | tf_op jit(solution)/shard_map/while/body/eval_jaxpr/while/body/eval_jaxpr/qhd,khd->hqk/dot_general | solution.py:68
  339.3 21.4 %multiply_convert_fusion.4 = bf16[8,512,1536]{2,1,0:T(8,128)(2,1)} fusion(f32[8,512,1536]{2,1,0:T(8,128)} %subtract_exponential_fusion.3, f32[8,512,1536]{2,1,0:T(8,128)} %get-tuple-element.517, f32[8,512]{1,0:T(8,128)S(1)} %get-tuple-element.518), kind=kLoop, calls=%fused_computation.15.clone.1 | loop fusion | flops 18874368 | bytes 62930944 | tf_op jit(solution)/shard_map/while/body/eval_jaxpr/while/body/eval_jaxpr/convert_element_type | solution.py:72
  360.7 9.7 fusion.137
  370.4 8.5 fusion.135
  386.0 13.2 subtract_exponential_fusion.3
  399.2 13.0 fusion.136
  412.3 16.5 %multiply_reduce_fusion.3 = (f32[8,512]{1,0:T(8,128)S(1)}, f32[8,512,1536]{2,1,0:T(8,128)}) fusion(f32[8,512,1536]{2,1,0:T(8,128)} %subtract_exponential_fusion.3, bf16[512,8,64]{0,2,1:T(8,128)(2,1)S(1)} %bitcast.169, bf16[1536,8,64]{0,2,1:T(8,128)(2,1)} %get-tuple-element.590), kind=kOutput, calls=%fused_computation.16.clone.1 | convolution fusion | flops 817885184 | bytes 52445184 | tf_op jit(solution)/shard_map/while/body/eval_jaxpr/while/body/eval_jaxpr/qhd,khd->hqk/dot_general | solution.py:68
  428.8 21.4 %multiply_convert_fusion.4 = bf16[8,512,1536]{2,1,0:T(8,128)(2,1)} fusion(f32[8,512,1536]{2,1,0:T(8,128)} %subtract_exponential_fusion.3, f32[8,512,1536]{2,1,0:T(8,128)} %get-tuple-element.517, f32[8,512]{1,0:T(8,128)S(1)} %get-tuple-element.518), kind=kLoop, calls=%fused_computation.15.clone.1 | loop fusion | flops 18874368 | bytes 62930944 | tf_op jit(solution)/shard_map/while/body/eval_jaxpr/while/body/eval_jaxpr/convert_element_type | solution.py:72
  450.1 9.7 fusion.137
  459.9 9.4 fusion.135
  476.4 13.2 subtract_exponential_fusion.3
  489.6 13.0 fusion.136
  502.6 16.5 %multiply_reduce_fusion.3 = (f32[8,512]{1,0:T(8,128)S(1)}, f32[8,512,1536]{2,1,0:T(8,128)}) fusion(f32[8,512,1536]{2,1,0:T(8,128)} %subtract_exponential_fusion.3, bf16[512,8,64]{0,2,1:T(8,128)(2,1)S(1)} %bitcast.169, bf16[1536,8,64]{0,2,1:T(8,128)(2,1)} %get-tuple-element.590), kind=kOutput, calls=%fused_computation.16.clone.1 | convolution fusion | flops 817885184 | bytes 52445184 | tf_op jit(solution)/shard_map/while/body/eval_jaxpr/while/body/eval_jaxpr/qhd,khd->hqk/dot_general | solution.py:68
  519.1 21.4 %multiply_convert_fusion.4 = bf16[8,512,1536]{2,1,0:T(8,128)(2,1)} fusion(f32[8,512,1536]{2,1,0:T(8,128)} %subtract_exponential_fusion.3, f32[8,512,1536]{2,1,0:T(8,128)} %get-tuple-element.517, f32[8,512]{1,0:T(8,128)S(1)} %get-tuple-element.518), kind=kLoop, calls=%fused_computation.15.clone.1 | loop fusion | flops 18874368 | bytes 62930944 | tf_op jit(solution)/shard_map/while/body/eval_jaxpr/while/body/eval_jaxpr/convert_element_type | solution.py:72
  540.5 9.7 fusion.137
  550.2 9.4 fusion.135
  573.6 9.0 fusion.38
  582.8 8.7 fusion.37
  591.6 11.0 fusion.52
  602.6 16.8 %fusion.26 = f32[1024,2816]{1,0:T(8,128)} fusion(bf16[1536,1408]{1,0:T(8,128)(2,1)} %get-tuple-element.364, bf16[1536,1408]{1,0:T(8,128)(2,1)} %copy-done.31, bf16[1536,1,1024]{2,0,1:T(8,128)(2,1)S(1)} %copy-done.29), kind=kOutput, calls=%fused_computation.57 | convolution fusion | flops 8875671552 | bytes 23330816 | tf_op jit(solution)/shard_map/lrd,lrf->df/dot_general | solution.py:179
  619.5 9.6 fusion.71
  629.1 7.3 fusion.58
  648.1 45.2 %all-reduce = (f32[1024]{0:T(1024)S(1)}, f32[1024]{0:T(1024)S(1)}) all-reduce(f32[1024]{0:T(1024)S(1)} %get-tuple-element.300, f32[1024]{0:T(1024)S(1)} %copy-done.26), channel_id=1, replica_groups=mesh['dp'=16,'mp'=2] {'dp'}, use_global_device_ids=true, to_apply=%region_23.24 | all-reduce | flops 2048 | bytes 16384 | tf_op jit(solution)/shard_map/psum | solution.py:246
  696.5 7.0 fusion.45
  703.5 628.5 %all-reduce.5.cloned.1.call-done = (f32[1024,512]{1,0:T(8,128)}, f32[1024,512]{1,0:T(8,128)}, f32[1024,512]{1,0:T(8,128)}, f32[512,1024]{1,0:T(8,128)}, f32[1024...) async-done(((f32[1024,512]{1,0:T(8,128)}, f32[1024,512]{1,0:T(8,128)}, f32[1024,512]{1,0:T(8,128)}, f32[512,1024]{1,0:T(8,128)}, f32[1024,1408]{1,0:T(8,128)}, ...) | async-done | bytes 25690128 | tf_op jit(solution)/shard_map/psum | solution.py:246
  (206 shorter events, 130.9 us)
Async XLA Ops:
  7.2 211.7 %copy-start = (bf16[1408,1024]{1,0:T(8,128)(2,1)S(1)}, bf16[1408,1024]{1,0:T(8,128)(2,1)}, u32[]{:S(2)}) copy-start(bf16[1408,1024]{1,0:T(8,128)(2,1)} %param.26) | copy-start | bytes 8650756
  7.2 6.3 copy-start.27
  7.2 6.3 copy-start.28
  7.2 21.2 %all-gather.5.cloned.1.call-start = ((), (), s32[]{:S(2)}) async-start(), calls=%async_computation.4 | async-start | bytes 4718592 | tf_op jit(solution)/shard_map/all_gather | solution.py:133
  13.4 170.3 %reduce-scatter.5.cloned.1.call-start = ((), (), s32[]{:S(2)}) async-start(), calls=%async_computation.5 | async-start | bytes 9437184 | tf_op jit(solution)/shard_map/reduce_scatter | solution.py:149
  13.5 4.6 copy-start.14
  45.5 1.8 copy-start.1
  57.9 11.8 copy-start.6
  84.1 1.8 copy-start.1
  96.6 11.8 copy-start.6
  122.8 1.8 copy-start.1
  135.3 11.8 copy-start.6
  167.8 20.3 %copy-start.17 = (f32[1024]{0:T(1024)S(1)}, f32[1024]{0:T(1024)}, u32[]{:S(2)}) copy-start(f32[1024]{0:T(1024)} %param.28) | copy-start | bytes 12292
  167.8 35.2 %all-gather.7.cloned.1.call-start = ((), (), s32[]{:S(2)}) async-start(), calls=%async_computation.6 | async-start | bytes 4718592 | tf_op jit(solution)/shard_map/all_gather | solution.py:156
  186.5 1.6 copy-start.2
  186.5 82.5 %copy-start.15 = (f32[768]{0:T(1024)}, f32[768]{0:T(1024)S(1)}, u32[]{:S(2)}) copy-start(f32[768]{0:T(1024)S(1)} %fusion.65) | copy-start | bytes 9220
  189.6 29.2 %all-gather.9.cloned.1.call-start = ((), (), s32[]{:S(2)}) async-start(), calls=%async_computation.8 | async-start | bytes 4718592 | tf_op jit(solution)/shard_map/all_gather | solution.py:172
  190.2 74.7 %reduce-scatter.9.cloned.1.call-start = ((), (), s32[]{:S(2)}) async-start(), calls=%async_computation.9 | async-start | bytes 4718592 | tf_op jit(solution)/shard_map/reduce_scatter | solution.py:183
  190.3 3.8 copy-start.8
  236.7 2.0 copy-start.31
  252.6 33.3 %all-gather.11.cloned.1.call-start = ((), (), s32[]{:S(2)}) async-start(), calls=%async_computation.10 | async-start | bytes 4718592 | tf_op jit(solution)/shard_map/all_gather | solution.py:195
  264.9 4.1 copy-start.3
  264.9 4.1 copy-start.7
  269.0 3.5 copy-start.24
  272.5 371.7 %reduce-scatter.11.cloned.1.call-start = ((), (), s32[]{:S(2)}) async-start(), calls=%async_computation.11 | async-start | bytes 4718592 | tf_op jit(solution)/shard_map/reduce_scatter | solution.py:223
  360.7 9.7 copy-start.5
  450.1 9.7 copy-start.5
  540.5 9.7 copy-start.5
  582.7 113.7 %reduce-scatter.7.cloned.1.call-start = ((), (), s32[]{:S(2)}) async-start(), calls=%async_computation.7 | async-start | bytes 4718592 | tf_op jit(solution)/shard_map/reduce_scatter | solution.py:162
  591.5 740.5 %all-reduce.5.cloned.1.call-start = ((), (), s32[]{:S(2)}) async-start(), calls=%async_computation.12 | async-start | bytes 51380224 | tf_op jit(solution)/shard_map/psum | solution.py:246
  591.6 11.1 copy-start.29
  619.4 9.7 copy-start.10
  619.4 9.7 copy-start.11
  619.5 9.7 copy-start.12
  636.4 3.3 copy-start.13
  636.5 4.6 copy-start.30
  644.2 3.9 copy-start.26
  644.2 52.2 %copy-start.22 = (f32[768]{0:T(1024)S(1)}, f32[768]{0:T(1024)}, u32[]{:S(2)}) copy-start(f32[768]{0:T(1024)} %copy-done.21) | copy-start | bytes 9220
  644.2 52.2 %copy-start.16 = (f32[768]{0:T(1024)S(1)}, f32[768]{0:T(1024)}, u32[]{:S(2)}) copy-start(f32[768]{0:T(1024)} %copy-done.15) | copy-start | bytes 9220
  644.2 52.2 %copy-start.18 = (f32[1024]{0:T(1024)S(1)}, f32[1024]{0:T(1024)}, u32[]{:S(2)}) copy-start(f32[1024]{0:T(1024)} %param.28) | copy-start | bytes 12292
  644.2 52.2 %copy-start.25 = (f32[768]{0:T(1024)S(1)}, f32[768]{0:T(1024)}, u32[]{:S(2)}) copy-start(f32[768]{0:T(1024)} %copy-done.24) | copy-start | bytes 9220
  1332.0 11.0 slice-start.4
  1335.2 10.7 slice-start.2
  1338.5 3.2 copy-start.9
  1338.5 4.6 slice-start.5
  1341.7 4.3 slice-start.3
  1343.0 5.8 slice-start
  1346.0 3.9 slice-start.1
  (7 other events, 4.9 us)
Sparse Core Ops, SparseCore 0:
  13.5 14.8 all-gather.4
  167.9 15.6 reduce-scatter.4
  189.7 13.2 all-gather.6
  204.5 13.2 all-gather.8
  252.8 12.0 reduce-scatter.8
  272.7 13.2 all-gather.10
  582.8 12.0 reduce-scatter.10
  597.3 12.0 reduce-scatter.6
  644.3 687.6 all-reduce.4
where the time goes:
time: 1370 us; the launch traced here: 1360 us
  waiting for transfers between devices  676 us (49%)
  matrix products  375 us (27%)
  other arithmetic  137 us (10%)
  local copies, waits for them, and re-layouts  97 us (7%)
  blocking collectives  48.3 us (4%)
  between operations  14.4 us (1%)
    psum x1, waiting for transfers between devices, shards(): lax.psum((grad_w_query, grad_w_key, grad_w_value, grad_w_out, grad_w_gate...  628 us
    dot_general x6, matrix products, masked_scores(): jnp.einsum('qhd,khd->hqk', query_heads, key_heads, preferred_element_type...  71.6 us
    convert_element_type x3, other arithmetic, single_block(): dscore = (probs * (dprob - spread)).astype(jnp.bfloat16)  64.2 us
    dot_general x3, matrix products, single_block(): jnp.einsum('qhd,khd->hqk', grad_heads, value_heads, preferred_element_typ...  49.5 us
    psum x1, blocking collectives, shards(): lax.psum((grad_w_query, grad_w_key, grad_w_value, grad_w_out, grad_w_gate...  45.2 us
    dot_general x3, matrix products, single_block(): jnp.einsum('hqk,qhd->khd', probs.astype(jnp.bfloat16), grad_heads, prefer...  38.2 us
    dot_general x3, matrix products, single_block(): jnp.einsum('hqk,khd->qhd', probs_low, value_heads, preferred_element_type...  36.8 us
    unnamed x78, local copies, waits for them, and re-layouts  35.6 us
  transfers between devices with their start and end apart: 9, of which 6 were waited for; matrix products, arithmetic and copies ran while one was open for 7% of the time, Pallas kernels for 0%

commit v1 on v0

v1 whole, which is shorter than its diff:
```python
import functools

import jax
import jax.numpy as jnp
from jax import lax
from jax.experimental import pallas as pl
from jax.experimental.pallas import tpu as pltpu
from jax.sharding import PartitionSpec as P

HDIM = 64
EPSILON = 1e-06
LOG2E = 1.4426950408889634
BF = jnp.bfloat16
F32 = jnp.float32
VMEM_LIMIT = 58 * 1024 * 1024
NN = ((1,), (0,))
NT = ((1,), (1,))
FFN_CHUNKS = (384, 512, 512)


def dot(left, right, dims=NN):
    return lax.dot_general(left, right, (dims, ((), ())), preferred_element_type=F32)


def params():
    return pltpu.CompilerParams(vmem_limit_bytes=VMEM_LIMIT)


def cost(flops, moved):
    return pl.CostEstimate(flops=flops, bytes_accessed=moved, transcendentals=0)


def shape(dims, dtype):
    return jax.ShapeDtypeStruct(dims, dtype)


def qkv_kernel(tokens, gain, wq, wk, wv, *refs):
    projected, normed_t = refs[-2:]
    x = tokens[...].astype(F32)
    r = lax.rsqrt(jnp.mean(x * x, axis=-1, keepdims=True) + EPSILON)
    low = (x * r * gain[...]).astype(BF)
    width = wq.shape[1]
    for at, w in enumerate((wq, wk, wv)):
        projected[:, at * width : (at + 1) * width] = dot(low, w[...]).astype(BF)
    normed_t[...] = low.T


def project(tokens, gain, wq, wk, wv, half, before=None):
    rows, d = tokens.shape
    width = wq.shape[1]
    tile = rows // 2
    whole = lambda a: pl.BlockSpec(a.shape, lambda i: (0, 0))
    args = [tokens, gain, wq, wk, wv]
    specs = [pl.BlockSpec((tile, d), lambda i: (i, 0))] + [whole(a) for a in args[1:]]
    alias = {}
    if before is not None:
        args += list(before)
        specs += [pl.BlockSpec(memory_space=pl.ANY)] * 2
        alias = {5: 0, 6: 1}
    return pl.pallas_call(
        qkv_kernel,
        grid=(2,),
        in_specs=specs,
        out_specs=[
            pl.BlockSpec((tile, 3 * width), lambda i: (i + 2 * half, 0)),
            pl.BlockSpec((d, tile), lambda i: (0, i + 2 * half)),
        ],
        out_shape=[shape((2 * rows, 3 * width), BF), shape((d, 2 * rows), BF)],
        input_output_aliases=alias,
        compiler_params=params(),
        cost_estimate=cost(2 * rows * d * 3 * width, 8 * rows * d),
    )(*args)


def slot_rows(meta, logical, slot):
    return pl.ds(pl.multiple_of(meta[logical] * slot, slot), slot)


def two_heads(columns):
    slot = columns.shape[1]
    zero = jnp.zeros((HDIM, slot), BF)
    first = jnp.concatenate([columns[:HDIM], zero], 0)
    second = jnp.concatenate([zero, columns[HDIM:]], 0)
    return jnp.concatenate([first, second], 1)


def attend_kernel(meta, q_ref, k_ref, v_ref, o_ref, ot_ref, lse_ref, *, slot):
    scale = HDIM**-0.5 * LOG2E
    padded = meta[4]
    rows = lambda logical: slot_rows(meta, logical, slot)

    def attend(at, key_slots):
        q2 = two_heads(q_ref[rows(at), :].T)
        scores = [dot(k_ref[rows(j), :], q2) for j in key_slots]
        top = functools.reduce(
            jnp.maximum, [jnp.max(s, axis=0, keepdims=True) for s in scores]
        )
        one = jnp.ones((16, slot), BF)
        oa = jnp.zeros((HDIM + 16, slot), F32)
        ob = oa
        for j, s in zip(key_slots, scores):
            p = jnp.exp2((s - top) * scale).astype(BF)
            vt = v_ref[rows(j), :].T
            oa += dot(jnp.concatenate([vt[:HDIM], one], 0), p[:, :slot])
            ob += dot(jnp.concatenate([vt[HDIM:], one], 0), p[:, slot:])
        la, lb = oa[HDIM : HDIM + 1], ob[HDIM : HDIM + 1]
        ot = jnp.concatenate([oa[:HDIM] / la, ob[:HDIM] / lb], 0).astype(BF)
        ot_ref[:, rows(at)] = ot
        o_ref[rows(at), :] = ot.T
        lse = top * HDIM**-0.5 + jnp.log(jnp.concatenate([la, lb], 1))
        lse_ref[0, 0:1, rows(at)] = lse[:, :slot]
        lse_ref[0, 1:2, rows(at)] = lse[:, slot:]

    lax.fori_loop(0, 3 + padded, lambda i, c: (attend(i, (0, 1, 2)), c)[1], 0)

    @pl.when(padded == 0)
    def _():
        attend(3, (3,))


def attend(meta, qkv):
    seq, width = qkv.shape[0], qkv.shape[1] // 3
    pairs = width // 128
    column = lambda off: pl.BlockSpec((seq, 128), lambda p, m: (0, p + off))
    return pl.pallas_call(
        functools.partial(attend_kernel, slot=seq // 4),
        grid_spec=pltpu.PrefetchScalarGridSpec(
            num_scalar_prefetch=1,
            grid=(pairs,),
            in_specs=[column(0), column(pairs), column(2 * pairs)],
            out_specs=[
                column(0),
                pl.BlockSpec((128, seq), lambda p, m: (p, 0)),
                pl.BlockSpec((1, 2, seq), lambda p, m: (p, 0, 0)),
            ],
        ),
        out_shape=[shape((seq, width), BF), shape((width, seq), BF), shape((pairs, 2, seq), F32)],
        compiler_params=params(),
        cost_estimate=cost(20 * seq * seq * width, 5 * seq * width * 2),
    )(meta, qkv, qkv, qkv)


def attend_back_kernel(
    meta, q_ref, k_ref, v_ref, ot_ref, do_ref, lse_ref, dq_ref, dk_ref, dv_ref, dk_sum, dv_sum, *, slot
):
    scale = HDIM**-0.5 * LOG2E
    padded = meta[4]
    rows = lambda logical: slot_rows(meta, logical, slot)
    lane = lax.broadcasted_iota(jnp.int32, (slot, 128), 1)
    ones = jnp.ones((slot, 128), BF)

    def stacked(x):
        zero = jnp.zeros_like(x)
        return jnp.concatenate([jnp.where(lane < HDIM, x, zero), jnp.where(lane < HDIM, zero, x)], 0)

    def extended(columns, tail):
        high = tail.astype(BF).astype(F32)
        rest = tail - high
        middle = rest.astype(BF).astype(F32)
        extra = jnp.concatenate(
            [high, middle, rest - middle, jnp.zeros((125, 2 * slot), F32)], 0
        ).astype(BF)
        return jnp.concatenate([two_heads(columns), extra], 0)

    def attend(at, key_slots, first):
        q, do = q_ref[rows(at), :], do_ref[rows(at), :]
        do_t = do.T
        prod = do_t.astype(F32) * ot_ref[:, rows(at)].astype(F32)
        delta = jnp.concatenate(
            [jnp.sum(prod[:HDIM], 0, keepdims=True), jnp.sum(prod[HDIM:], 0, keepdims=True)], 1
        )
        lse = jnp.concatenate([lse_ref[0, 0:1, rows(at)], lse_ref[0, 1:2, rows(at)]], 1)
        q2 = extended(q.T, lse * -(HDIM**0.5))
        do2 = extended(do_t, -delta)
        qs, dos = stacked(q), stacked(do)
        dqa = jnp.zeros((HDIM, slot), F32)
        dqb = dqa
        for j in key_slots:
            k, v = k_ref[rows(j), :], v_ref[rows(j), :]
            p = jnp.exp2(dot(jnp.concatenate([k, ones], 1), q2) * scale)
            dp = dot(jnp.concatenate([v, ones], 1), do2)
            ds = (p * dp).astype(BF)
            dv = dot(p.astype(BF), dos)
            dk = dot(ds, qs)
            kt = k.T
            dqa += dot(kt[:HDIM], ds[:, :slot])
            dqb += dot(kt[HDIM:], ds[:, slot:])
            if first:
                dk_sum[rows(j), :] = dk
                dv_sum[rows(j), :] = dv
            else:
                dk_sum[rows(j), :] += dk
                dv_sum[rows(j), :] += dv
        dq_ref[rows(at), :] = (jnp.concatenate([dqa, dqb], 0) * HDIM**-0.5).astype(BF).T

    dk_sum[...] = jnp.zeros_like(dk_sum)
    dv_sum[...] = jnp.zeros_like(dv_sum)
    lax.fori_loop(0, 3 + padded, lambda i, c: (attend(i, (0, 1, 2), False), c)[1], 0)

    @pl.when(padded == 0)
    def _():
        attend(3, (3,), True)

    dk_ref[...] = (dk_sum[...] * HDIM**-0.5).astype(BF)
    dv_ref[...] = dv_sum[...].astype(BF)


def attend_back(meta, qkv, mixed_t, grad_mixed, lse):
    seq, width = qkv.shape[0], qkv.shape[1] // 3
    pairs = width // 128
    column = lambda off: pl.BlockSpec((seq, 128), lambda p, m: (0, p + off))
    return pl.pallas_call(
        functools.partial(attend_back_kernel, slot=seq // 4),
        grid_spec=pltpu.PrefetchScalarGridSpec(
            num_scalar_prefetch=1,
            grid=(pairs,),
            in_specs=[
                column(0),
                column(pairs),
                column(2 * pairs),
                pl.BlockSpec((128, seq), lambda p, m: (p, 0)),
                column(0),
                pl.BlockSpec((1, 2, seq), lambda p, m: (p, 0, 0)),
            ],
            out_specs=[column(0)] * 3,
            scratch_shapes=[pltpu.VMEM((seq, 128), F32)] * 2,
        ),
        out_shape=[shape((seq, width), BF)] * 3,
        compiler_params=params(),
        cost_estimate=cost(30 * seq * seq * width, 8 * seq * width * 2),
    )(meta, qkv, qkv, qkv, mixed_t, grad_mixed, lse)


def matmul_kernel(a, b, out, *, dims):
    out[...] = dot(a[...], b[...], dims).astype(out.dtype)


def matmul_rows(a, b, dims, dtype, tile=256):
    rows, depth = a.shape
    width = b.shape[1] if dims == NN else b.shape[0]
    return pl.pallas_call(
        functools.partial(matmul_kernel, dims=dims),
        grid=(rows // tile,),
        in_specs=[pl.BlockSpec((tile, depth), lambda i: (i, 0)), pl.BlockSpec(b.shape, lambda i: (0, 0))],
        out_specs=pl.BlockSpec((tile, width), lambda i: (i, 0)),
        out_shape=shape((rows, width), dtype),
        compiler_params=params(),
        cost_estimate=cost(2 * rows * depth * width, 2 * (rows * depth + depth * width + rows * width)),
    )(a, b)


def middle_kernel(own, other, mine, theirs, gain, hidden, normed, normed_t):
    tokens = jnp.where(pl.program_id(0) < pl.num_programs(0) // 2, own[...], other[...]).astype(F32)
    h = tokens + (mine[...].astype(F32) + theirs[...].astype(F32))
    r = lax.rsqrt(jnp.mean(h * h, axis=-1, keepdims=True) + EPSILON)
    low = (h * r * gain[...]).astype(BF)
    hidden[...] = h
    normed[...] = low
    normed_t[...] = low.T


def middle(own, other, mine, theirs, gain, tile=256):
    half, d = own.shape
    n = 2 * half // tile
    block = lambda f: pl.BlockSpec((tile, d), lambda i: (f(i), 0))
    return pl.pallas_call(
        middle_kernel,
        grid=(n,),
        in_specs=[
            block(lambda i: jnp.minimum(i, n // 2 - 1)),
            block(lambda i: jnp.maximum(i - n // 2, 0)),
            block(lambda i: i),
            block(lambda i: lax.rem(i + n // 2, n)),
            pl.BlockSpec((1, d), lambda i: (0, 0)),
        ],
        out_specs=[block(lambda i: i), block(lambda i: i), pl.BlockSpec((d, tile), lambda i: (0, i))],
        out_shape=[shape((2 * half, d), F32), shape((2 * half, d), BF), shape((d, 2 * half), BF)],
        compiler_params=params(),
        cost_estimate=cost(20 * half * d, 30 * half * d),
    )(own, other, mine, theirs, gain)


def gelu_parts(v):
    c = 0.7978845608028654
    t = jnp.tanh(c * (v + 0.044715 * v * v * v))
    value = 0.5 * v * (1.0 + t)
    slope = 0.5 * (1.0 + t) + 0.5 * v * (1.0 - t * t) * (c * (1.0 + 3 * 0.044715 * v * v))
    return value, slope


def ffn_kernel(quarters, x, ct, xt, ctq, wg, wu, wd, act, gg, gu, grads, both, act_t):
    at = pl.program_id(0)
    rows, width = act.shape

    @pl.when(at < 4)
    def _():
        gate = dot(x[...], wg[...])
        up = dot(x[...], wu[...])
        grad_act = dot(ct[...], wd[...], NT)
        value, slope = gelu_parts(gate)
        low = (value * up).astype(BF)
        grad_gate = (grad_act * up * slope).astype(BF)
        grad_up = (grad_act * value).astype(BF)
        act[...] = low
        gg[...] = grad_gate
        gu[...] = grad_up
        here = pl.ds(pl.multiple_of(at * rows, rows), rows)
        both[here, :width] = grad_gate
        both[here, width:] = grad_up
        act_t[:, here] = low.T

    @pl.when(at >= 4)
    def _():
        grads[0, :, : 2 * width] = dot(xt[...], both[...]).astype(BF)
        down = dot(act_t[...], ctq[...]).astype(BF)
        for i in range(width // 128):
            tile = down[i * 128 : (i + 1) * 128]
            grads[0, :128, i * 128 + 2 * width : (i + 1) * 128 + 2 * width] = tile[:, :128]
            grads[0, 128:, i * 128 + 2 * width : (i + 1) * 128 + 2 * width] = tile[:, 128:]


def ffn(quarters, x, ct, xt, wg, wu, wd):
    seq, d = x.shape
    width = wg.shape[1]
    tile = seq // 4
    early = lambda s, q: jnp.minimum(s, 3)
    late = lambda s, q: q[jnp.maximum(s - 4, 0)]
    rows = pl.BlockSpec((tile, d), lambda s, q: (early(s, q), 0))
    low = pl.BlockSpec((tile, width), lambda s, q: (early(s, q), 0))
    return pl.pallas_call(
        ffn_kernel,
        grid_spec=pltpu.PrefetchScalarGridSpec(
            num_scalar_prefetch=1,
            grid=(8,),
            in_specs=[
                rows,
                rows,
                pl.BlockSpec((d // 4, seq), lambda s, q: (late(s, q), 0)),
                pl.BlockSpec((seq, d // 4), lambda s, q: (0, late(s, q))),
                pl.BlockSpec((d, width), lambda s, q: (0, 0)),
                pl.BlockSpec((d, width), lambda s, q: (0, 0)),
                pl.BlockSpec((width, d), lambda s, q: (0, 0)),
            ],
            out_specs=[
                low,
                low,
                low,
                pl.BlockSpec((1, d // 4, 3 * width), lambda s, q: (jnp.maximum(s - 4, 0), 0, 0)),
            ],
            scratch_shapes=[pltpu.VMEM((seq, 2 * width), BF), pltpu.VMEM((width, seq), BF)],
        ),
        out_shape=[shape((seq, width), BF)] * 3 + [shape((4, d // 4, 3 * width), BF)],
        compiler_params=params(),
        cost_estimate=cost(12 * seq * d * width, 8 * seq * d + 12 * d * width),
    )(quarters, x, ct, xt, ct, wg, wu, wd)


def ffn_sums_kernel(*refs, chunks):
    acts, ggs, gus = refs[:chunks], refs[chunks : 2 * chunks], refs[2 * chunks : 3 * chunks]
    wg, wu, wd, own, send, back = refs[3 * chunks :]
    act = jnp.concatenate([a[...] for a in acts], 1)
    out = dot(act, wd[...])
    gg = jnp.concatenate([a[...] for a in ggs], 1)
    gu = jnp.concatenate([a[...] for a in gus], 1)
    back[...] = (dot(gg, wg[...], NT) + dot(gu, wu[...], NT)).astype(BF)
    late = pl.program_id(0) >= pl.num_programs(0) // 2

    @pl.when(late)
    def _():
        own[...] = out

    @pl.when(jnp.logical_not(late))
    def _():
        send[...] = out.astype(BF)


def ffn_sums(acts, ggs, gus, wg, wu, wd, tile=256):
    seq, d = acts[0].shape[0], wd.shape[1]
    n = seq // tile
    row = lambda i: lax.rem(i + n // 2, n)
    whole = lambda a: pl.BlockSpec(a.shape, lambda i: (0, 0))
    return pl.pallas_call(
        functools.partial(ffn_sums_kernel, chunks=len(acts)),
        grid=(n,),
        in_specs=[pl.BlockSpec((tile, a.shape[1]), lambda i: (row(i), 0)) for a in acts + ggs + gus]
        + [whole(wg), whole(wu), whole(wd)],
        out_specs=[
            pl.BlockSpec((tile, d), lambda i: (jnp.maximum(i - n // 2, 0), 0)),
            pl.BlockSpec((tile, d), lambda i: (jnp.minimum(i, n // 2 - 1), 0)),
            pl.BlockSpec((tile, d), lambda i: (row(i), 0)),
        ],
        out_shape=[shape((seq // 2, d), F32), shape((seq // 2, d), BF), shape((seq, d), BF)],
        compiler_params=params(),
        cost_estimate=cost(6 * seq * d * wg.shape[1], 10 * seq * d + 6 * d * wg.shape[1]),
    )(*acts, *ggs, *gus, wg, wu, wd)


def norm_back(value, gain, grad):
    r = lax.rsqrt(jnp.mean(value * value, axis=-1, keepdims=True) + EPSILON)
    u = grad * gain
    inner = jnp.mean(u * value, axis=-1, keepdims=True)
    return r * u - value * (r * r * r * inner), jnp.sum(grad * value * r, axis=0, keepdims=True)


def middle_back_kernel(mine, theirs, hidden, ct, gain, low, keep, gain_grad):
    at = pl.program_id(0)
    grad = mine[...].astype(F32) + theirs[...].astype(F32)
    through, part = norm_back(hidden[...], gain[...], grad)
    total = ct[...].astype(F32) + through
    low[...] = total.astype(BF)

    @pl.when(at == 0)
    def _():
        gain_grad[...] = part

    @pl.when(at > 0)
    def _():
        gain_grad[...] += part

    @pl.when(at < pl.num_programs(0) // 2)
    def _():
        keep[...] = total


def middle_back(mine, theirs, hidden, ct, gain, tile=256):
    seq, d = hidden.shape
    n = seq // tile
    block = lambda f: pl.BlockSpec((tile, d), lambda i: (f(i), 0))
    return pl.pallas_call(
        middle_back_kernel,
        grid=(n,),
        in_specs=[
            block(lambda i: i),
            block(lambda i: lax.rem(i + n // 2, n)),
            block(lambda i: i),
            block(lambda i: i),
            pl.BlockSpec((1, d), lambda i: (0, 0)),
        ],
        out_specs=[
            block(lambda i: i),
            block(lambda i: jnp.minimum(i, n // 2 - 1)),
            pl.BlockSpec((1, d), lambda i: (0, 0)),
        ],
        out_shape=[shape((seq, d), BF), shape((seq // 2, d), F32), shape((1, d), F32)],
        compiler_params=params(),
        cost_estimate=cost(20 * seq * d, 14 * seq * d),
    )(mine, theirs, hidden, ct, gain)


def out_back_kernel(quarters, g, gq, mixed_t, w_out, grad_mixed, grads):
    at = pl.program_id(0)

    @pl.when(at < 4)
    def _():
        grad_mixed[...] = dot(g[...], w_out[...], NT).astype(BF)

    @pl.when(at >= 4)
    def _():
        part = dot(mixed_t[...], gq[...]).astype(BF)
        step = grads.shape[1]
        for i in range(part.shape[0] // step):
            grads[0, :, i * part.shape[1] : (i + 1) * part.shape[1]] = part[i * step : (i + 1) * step]


def out_back(quarters, g, mixed_t, w_out):
    seq, d = g.shape
    width = w_out.shape[0]
    late = lambda s, q: q[jnp.maximum(s - 4, 0)]
    return pl.pallas_call(
        out_back_kernel,
        grid_spec=pltpu.PrefetchScalarGridSpec(
            num_scalar_prefetch=1,
            grid=(8,),
            in_specs=[
                pl.BlockSpec((seq // 4, d), lambda s, q: (jnp.minimum(s, 3), 0)),
                pl.BlockSpec((seq, d // 4), lambda s, q: (0, late(s, q))),
                pl.BlockSpec((width, seq), lambda s, q: (0, 0)),
                pl.BlockSpec((width, d), lambda s, q: (0, 0)),
            ],
            out_specs=[
                pl.BlockSpec((seq // 4, width), lambda s, q: (jnp.minimum(s, 3), 0)),
                pl.BlockSpec((1, d // 4, width), lambda s, q: (jnp.maximum(s - 4, 0), 0, 0)),
            ],
        ),
        out_shape=[shape((seq, width), BF), shape((4, d // 4, width), BF)],
        compiler_params=params(),
        cost_estimate=cost(4 * seq * d * width, 6 * seq * d),
    )(quarters, g, g, mixed_t, w_out)


def qkv_grads_kernel(quarters, normed_t, dq, dk, dv, grads):
    width = dq.shape[1]
    for at, part in enumerate((dq, dk, dv)):
        grads[0, :, at * width : (at + 1) * width] = dot(normed_t[...], part[...]).astype(BF)


def qkv_grads(quarters, normed_t, dq, dk, dv):
    d, seq = normed_t.shape
    width = dq.shape[1]
    whole = pl.BlockSpec((seq, width), lambda s, q: (0, 0))
    return pl.pallas_call(
        qkv_grads_kernel,
        grid_spec=pltpu.PrefetchScalarGridSpec(
            num_scalar_prefetch=1,
            grid=(4,),
            in_specs=[pl.BlockSpec((d // 4, seq), lambda s, q: (q[s], 0)), whole, whole, whole],
            out_specs=pl.BlockSpec((1, d // 4, 3 * width), lambda s, q: (s, 0, 0)),
        ),
        out_shape=shape((4, d // 4, 3 * width), BF),
        compiler_params=params(),
        cost_estimate=cost(6 * seq * d * width, 8 * seq * d),
    )(quarters, normed_t, dq, dk, dv)


def qkv_back_kernel(dq, dk, dv, wq, wk, wv, own, send):
    total = dot(dq[...], wq[...], NT) + dot(dk[...], wk[...], NT) + dot(dv[...], wv[...], NT)
    late = pl.program_id(0) >= pl.num_programs(0) // 2

    @pl.when(late)
    def _():
        own[...] = total

    @pl.when(jnp.logical_not(late))
    def _():
        send[...] = total.astype(BF)


def qkv_back(dq, dk, dv, wq, wk, wv, tile=256):
    seq, width = dq.shape
    d = wq.shape[0]
    n = seq // tile
    rows = pl.BlockSpec((tile, width), lambda i: (lax.rem(i + n // 2, n), 0))
    whole = pl.BlockSpec((d, width), lambda i: (0, 0))
    return pl.pallas_call(
        qkv_back_kernel,
        grid=(n,),
        in_specs=[rows] * 3 + [whole] * 3,
        out_specs=[
            pl.BlockSpec((tile, d), lambda i: (jnp.maximum(i - n // 2, 0), 0)),
            pl.BlockSpec((tile, d), lambda i: (jnp.minimum(i, n // 2 - 1), 0)),
        ],
        out_shape=[shape((seq // 2, d), F32), shape((seq // 2, d), BF)],
        compiler_params=params(),
        cost_estimate=cost(6 * seq * d * width, 12 * seq * d),
    )(dq, dk, dv, wq, wk, wv)


def last_kernel(mine, theirs, tokens, grad_hidden, gain, out, gain_grad):
    at = pl.program_id(0)
    through, part = norm_back(
        tokens[...].astype(F32), gain[...], mine[...] + theirs[...].astype(F32)
    )
    out[...] = (grad_hidden[...] + through).astype(BF)

    @pl.when(at == 0)
    def _():
        gain_grad[...] = part

    @pl.when(at > 0)
    def _():
        gain_grad[...] += part


def last(mine, theirs, tokens, grad_hidden, gain, tile=256):
    rows, d = tokens.shape
    block = pl.BlockSpec((tile, d), lambda i: (i, 0))
    one = pl.BlockSpec((1, d), lambda i: (0, 0))
    return pl.pallas_call(
        last_kernel,
        grid=(rows // tile,),
        in_specs=[block] * 4 + [one],
        out_specs=[block, one],
        out_shape=[shape((rows, d), BF), shape((1, d), F32)],
        compiler_params=params(),
        cost_estimate=cost(20 * rows * d, 16 * rows * d),
    )(mine, theirs, tokens, grad_hidden, gain)


def swap(x):
    return lax.ppermute(x, "mp", [(0, 1), (1, 0)])


def down_layout(part):
    four, rows, width = part.shape
    tiles = part.reshape(four, rows // 128, 128, width // 128, 128)
    return tiles.transpose(3, 2, 0, 1, 4).reshape(width, four * rows)


def shards(
    tokens,
    segment_ids,
    keep_mask,
    w_query,
    w_key,
    w_value,
    w_out,
    w_gate,
    w_up,
    w_down,
    norm_attn,
    norm_ffn,
    cotangent,
):
    half, d = tokens.shape[0], tokens.shape[2]
    seq = segment_ids.shape[1]
    slot = seq // 4
    core = lax.axis_index("mp")
    segs, keep = segment_ids[0], keep_mask[0]
    middle_at = seq // 2
    leads = (segs[0] != segs[middle_at]) | (keep[0] == 0)
    ends = (segs[seq - 1] != segs[middle_at]) | (keep[seq - 1] == 0)
    start = jnp.where(leads, 1, 0)
    padded = jnp.where(jnp.where(leads, keep[0], keep[seq - 1]) == 0, 1, 0)
    logical = (jnp.arange(4, dtype=jnp.int32) + start) % 4
    meta = jnp.concatenate([(logical + 2 * core) % 4, padded[None]]).astype(jnp.int32)
    quarters = jnp.arange(4, dtype=jnp.int32)

    own = tokens[:, 0]
    ct_own = cotangent[:, 0]
    gain_attn, gain_ffn = norm_attn[None], norm_ffn[None]
    other = swap(own)
    ct = jnp.concatenate([ct_own, swap(ct_own)], 0)
    first = project(own, gain_attn, w_query, w_key, w_value, 0)
    qkv, normed_t = project(other, gain_attn, w_query, w_key, w_value, 1, first)
    mixed, mixed_t, lse = attend(meta, qkv)
    attn_part = matmul_rows(mixed, w_out, NN, BF)
    hidden, x, xt = middle(own, other, attn_part, swap(attn_part), gain_ffn)

    acts, ggs, gus, ffn_grads = [], [], [], []
    at = 0
    for width in FFN_CHUNKS:
        a, gg, gu, grads = ffn(
            quarters, x, ct, xt, w_gate[:, at : at + width], w_up[:, at : at + width], w_down[at : at + width]
        )
        acts.append(a)
        ggs.append(gg)
        gus.append(gu)
        ffn_grads.append(lax.psum(grads, "dp"))
        at += width
    out_own, out_send, back_part = ffn_sums(acts, ggs, gus, w_gate, w_up, w_down)
    result = (hidden[:half] + (out_own + swap(out_send).astype(F32))).astype(BF)
    grad_in, grad_hidden, gain_ffn_part = middle_back(back_part, swap(back_part), hidden, ct, gain_ffn)
    grad_mixed, out_grads = out_back(quarters, grad_in, mixed_t, w_out)
    dq, dk, dv = attend_back(meta, qkv, mixed_t, grad_mixed, lse)
    attn_grads = qkv_grads(quarters, normed_t, dq, dk, dv)
    back_own, back_send = qkv_back(dq, dk, dv, w_query, w_key, w_value)
    grad_tokens, gain_attn_part = last(back_own, swap(back_send), own, grad_hidden, gain_attn)

    out_grads, attn_grads = lax.psum((out_grads, attn_grads), "dp")
    gain_attn_grad = lax.psum(gain_attn_part[0], ("dp", "mp"))
    gain_ffn_grad = lax.psum(gain_ffn_part[0], "dp")

    def columns(part):
        return part.reshape(d, -1).astype(F32)

    grad_gate = jnp.concatenate([columns(g[:, :, :w]) for g, w in zip(ffn_grads, FFN_CHUNKS)], 1)
    grad_up = jnp.concatenate([columns(g[:, :, w : 2 * w]) for g, w in zip(ffn_grads, FFN_CHUNKS)], 1)
    grad_down = jnp.concatenate(
        [down_layout(g[:, :, 2 * w :]).astype(F32) for g, w in zip(ffn_grads, FFN_CHUNKS)], 0
    )
    width = w_query.shape[1]
    quarter = d // 4
    grad_out = (
        out_grads.reshape(4, quarter, width // quarter, quarter)
        .transpose(2, 1, 0, 3)
        .reshape(width, d)
        .astype(F32)
    )
    return (
        result[:, None],
        grad_tokens[:, None],
        columns(attn_grads[:, :, :width]),
        columns(attn_grads[:, :, width : 2 * width]),
        columns(attn_grads[:, :, 2 * width :]),
        grad_out,
        grad_gate,
        grad_up,
        grad_down,
        gain_attn_grad,
        gain_ffn_grad,
    )


def solution(mesh):
    return jax.shard_map(
        shards,
        mesh=mesh,
        in_specs=(
            P("mp", "dp", None),
            P("dp", None),
            P("dp", None),
            P(None, "mp"),
            P(None, "mp"),
            P(None, "mp"),
            P("mp", None),
            P(None, "mp"),
            P(None, "mp"),
            P("mp", None),
            P(),
            P(),
            P("mp", "dp", None),
        ),
        out_specs=(
            P("mp", "dp", None),
            P("mp", "dp", None),
            P(None, "mp"),
            P(None, "mp"),
            P(None, "mp"),
            P("mp", None),
            P(None, "mp"),
            P(None, "mp"),
            P("mp", None),
            P(),
            P(),
        ),
        check_vma=False,
    )
```

time: 1370 us -> 687 us (0.50)
  waiting for transfers between devices: 676 us -> 263 us
  matrix products: 375 us -> 0 us
  Pallas kernels: 0 us -> 231 us
  other arithmetic: 137 us -> 22.3 us
  local copies, waits for them, and re-layouts: 97 us -> 54.3 us
  blocking collectives: 48.3 us -> 87.7 us
    dot_general x33 -> x0, matrix products: 375 us -> none  [the longest x6 71.6 us: masked_scores(): jnp.einsum('qhd,khd->hqk', query_heads, key_heads, preferred_element_type...]
    psum x1, waiting for transfers between devices: 628 us -> 257 us  [shards(): out_grads, attn_grads = lax.psum((out_grads, attn_grads), 'dp')]
    pallas_call x0 -> x15, Pallas kernels: none -> 231 us  [the longest x3 51.8 us: ffn(): pl.pallas_call(ffn_kernel, grid_spec=pltpu.PrefetchScalarGridSpec(num_sca...]
    convert_element_type x9 -> x4, other arithmetic: 85.6 us -> 6.61 us  [the longest x3 5.04 us: columns(): return part.reshape(d, -1).astype(F32)]
    reduce_sum x7 -> x0, other arithmetic: 47.5 us -> none  [the longest x3 35.3 us: single_block(): summed = jnp.sum(raised, axis=-1, keepdims=True)]
    psum x2, blocking collectives: 48.3 us -> 87.7 us  [the longest x1 46.3 us: shards(): gain_ffn_grad = lax.psum(gain_ffn_part[0], 'dp')]
    all_gather x4 -> x0, waiting for transfers between devices: 29.8 us -> none  [the longest x1 13.4 us: shards(): lax.all_gather(grad_hidden.astype(jnp.bfloat16), 'mp', axis=0, tiled=True)]
    unnamed x78 -> x33, local copies, waits for them, and re-layouts: 35.6 us -> 7.25 us
  transfers between devices with their start and end apart: 9 -> 7, of which waited for: 6 -> 2; matrix products, arithmetic and copies ran while one was open for 7% -> 3% of each run, Pallas kernels for 0% -> 5%
where the time goes in v1:
time: 687 us; the launch traced here: 677 us
  waiting for transfers between devices  263 us (38%)
  Pallas kernels  231 us (34%)
  blocking collectives  87.7 us (13%)
  local copies, waits for them, and re-layouts  54.3 us (8%)
  other arithmetic  22.3 us (3%)
  between operations  17.6 us (3%)
    psum x1, waiting for transfers between devices, shards(): out_grads, attn_grads = lax.psum((out_grads, attn_grads), 'dp')  257 us
    pallas_call x3, Pallas kernels, ffn(): pl.pallas_call(ffn_kernel, grid_spec=pltpu.PrefetchScalarGridSpec(num_sca...  51.8 us
    psum x1, blocking collectives, shards(): gain_ffn_grad = lax.psum(gain_ffn_part[0], 'dp')  46.3 us
    pallas_call x1, Pallas kernels, attend_back(): pl.pallas_call(functools.partial(attend_back_kernel, slot=seq // 4), grid...  42.7 us
    psum x1, blocking collectives, shards(): gain_attn_grad = lax.psum(gain_attn_part[0], ('dp', 'mp'))  41.4 us
    pallas_call x1, Pallas kernels, attend(): pl.pallas_call(functools.partial(attend_kernel, slot=seq // 4), grid_spec...  27.5 us
    pallas_call x1, Pallas kernels, ffn_sums(): pl.pallas_call(functools.partial(ffn_sums_kernel, chunks=len(acts)), grid...  22.3 us
    pallas_call x1, Pallas kernels, qkv_back(): pl.pallas_call(qkv_back_kernel, grid=(n,), in_specs=[rows] * 3 + [whole]...  19.7 us
  transfers between devices with their start and end apart: 7, of which 2 were waited for; matrix products, arithmetic and copies ran while one was open for 3% of the time, Pallas kernels for 5%

profile of v1, /device:TPU:0, one launch (start us, length us, event | category | flops | bytes accessed | tf_op | source)
XLA Modules:
  0.0 676.8 jit_solution(16979461423870157825)
XLA Ops:
  10.2 1.3 fusion.11
  14.1 6.4 shard_map.212
  21.6 6.4 shard_map.213
  28.1 27.5 %shard_map.214 = (bf16[1536,512]{1,0:T(8,128)(2,1)}, bf16[512,1536]{1,0:T(8,128)(2,1)}, f32[4,2,1536]{2,1,0:T(2,128)}) custom-call(s32[5]{0:T(128)} %pad_add_fusion.meta, bf16[1536,1536]{1,0:T(8,128)(2,1)} %get-tuple-element.50.q_ref.k_ref.v_ref, bf16[1536,1536]{1,0:T(8,128)(2,1)} %get-tuple-element.50.q_ref.k_ref.v_ref, ...), custom_call_target="tpu_custom_call" | custom-call | flops 24159191040 | bytes 7864320 | tf_op jit(solution)/shard_map/pallas_call | solution.py:125
  55.6 6.5 shard_map.215.mine
  62.6 2.1 slice.88.wg
  64.7 2.1 slice.89.wu
  67.8 1.6 fusion.7
  69.4 1.2 copy-done.12
  70.6 2.1 fusion.8
  72.9 2.0 pad_maximum_fusion.ct.ctq
  74.9 1.7 copy-done.8
  76.6 9.9 %shard_map.216 = (f32[1536,1024]{1,0:T(8,128)}, bf16[1536,1024]{1,0:T(8,128)(2,1)}, bf16[1024,1536]{1,0:T(8,128)(2,1)}) custom-call(bf16[768,1024]{1,0:T(8,128)(2,1)} %bitcast.39, bf16[768,1024]{1,0:T(8,128)(2,1)} %copy-done, bf16[1536,1024]{1,0:T(8,128)(2,1)} %shard_map.215.mine, bf16[1536,1024]{1,0:T(8,128)(2,1)} %copy-done.8, f32[1,1024]{1,0:T(1,128)} %bitcast.55), custom_call_target="tpu_custom_call" | custom-call | flops 15728640 | bytes 23592960 | tf_op jit(solution)/shard_map/pallas_call | solution.py:266
  87.1 17.7 %shard_map.219 = (bf16[1536,512]{1,0:T(8,128)(2,1)}, bf16[1536,512]{1,0:T(8,128)(2,1)}, bf16[1536,512]{1,0:T(8,128)(2,1)}, bf16[4,256,1536]{2,1,0:T(8,128)(2,1)}) custom-call(s32[4]{0:T(128)} %iota.17.quarters, bf16[1536,1024]{1,0:T(8,128)(2,1)} %get-tuple-element.53.x, bf16[1536,1024]{1,0:T(8,128)(2,1)} %pad_maximum_fusion.ct.ctq, ...), custom_call_target="tpu_custom_call" | custom-call | flops 9663676416 | bytes 18874368 | tf_op jit(solution)/shard_map/pallas_call | solution.py:330
  105.2 17.7 %shard_map.218 = (bf16[1536,512]{1,0:T(8,128)(2,1)}, bf16[1536,512]{1,0:T(8,128)(2,1)}, bf16[1536,512]{1,0:T(8,128)(2,1)}, bf16[4,256,1536]{2,1,0:T(8,128)(2,1)}) custom-call(s32[4]{0:T(128)} %iota.16.quarters, bf16[1536,1024]{1,0:T(8,128)(2,1)} %get-tuple-element.53.x, bf16[1536,1024]{1,0:T(8,128)(2,1)} %pad_maximum_fusion.ct.ctq, ...), custom_call_target="tpu_custom_call" | custom-call | flops 9663676416 | bytes 18874368 | tf_op jit(solution)/shard_map/pallas_call | solution.py:330
  123.4 16.4 %shard_map.217 = (bf16[1536,384]{1,0:T(8,128)(2,1)}, bf16[1536,384]{1,0:T(8,128)(2,1)}, bf16[1536,384]{1,0:T(8,128)(2,1)}, bf16[4,256,1152]{2,1,0:T(8,128)(2,1)}) custom-call(s32[4]{0:T(128)} %iota.15.quarters, bf16[1536,1024]{1,0:T(8,128)(2,1)} %get-tuple-element.53.x, bf16[1536,1024]{1,0:T(8,128)(2,1)} %pad_maximum_fusion.ct.ctq, ...), custom_call_target="tpu_custom_call" | custom-call | flops 7247757312 | bytes 17301504 | tf_op jit(solution)/shard_map/pallas_call | solution.py:330
  139.9 22.3 %shard_map.220 = (f32[768,1024]{1,0:T(8,128)}, bf16[768,1024]{1,0:T(8,128)(2,1)}, bf16[1536,1024]{1,0:T(8,128)(2,1)}) custom-call(bf16[1536,384]{1,0:T(8,128)(2,1)} %get-tuple-element.55.refs_0_, bf16[1536,512]{1,0:T(8,128)(2,1)} %get-tuple-element.56.refs_1_, bf16[1536,512]{1,0:T(8,128)(2,1)} %get-tuple-element.57.refs_2_, ...), custom_call_target="tpu_custom_call" | custom-call | flops 13287555072 | bytes 24379392 | tf_op jit(solution)/shard_map/pallas_call | solution.py:382
  162.3 5.8 collective-permute-done.4.theirs
  168.1 1.7 copy-done.9
  169.9 10.7 %shard_map.221 = (bf16[1536,1024]{1,0:T(8,128)(2,1)}, f32[768,1024]{1,0:T(8,128)}, f32[1,1024]{1,0:T(1,128)}) custom-call(bf16[1536,1024]{1,0:T(8,128)(2,1)} %get-tuple-element.67.mine, bf16[1536,1024]{1,0:T(8,128)(2,1)} %copy-done.9, f32[1536,1024]{1,0:T(8,128)} %get-tuple-element.52.hidden, bf16[1536,1024]{1,0:T(8,128)(2,1)} %pad_maximum_fusion.ct.ctq, ...), custom_call_target="tpu_custom_call" | custom-call | flops 31457280 | bytes 22020096 | tf_op jit(solution)/shard_map/pallas_call | solution.py:429
  181.1 10.6 %shard_map.222 = (bf16[1536,512]{1,0:T(8,128)(2,1)}, bf16[4,256,512]{2,1,0:T(8,128)(2,1)}) custom-call(s32[4]{0:T(128)} %iota.18.quarters, bf16[1536,1024]{1,0:T(8,128)(2,1)} %get-tuple-element.68.g.gq, bf16[1536,1024]{1,0:T(8,128)(2,1)} %get-tuple-element.68.g.gq, bf16[512,1536]{1,0:T(8,128)(2,1)} %get-tuple-element.66.mixed_t.ot_ref, bf16[512,1024]{1,0:T(8,128)(2,1)} %w_out.1), custom_call_target="tpu_custom_call" | custom-call | flops 3221225472 | bytes 9437184 | tf_op jit(solution)/shard_map/pallas_call | solution.py:469
  191.6 1.3 convert_element_type.98
  195.0 42.7 %shard_map.223 = (bf16[1536,512]{1,0:T(8,128)(2,1)}, bf16[1536,512]{1,0:T(8,128)(2,1)}, bf16[1536,512]{1,0:T(8,128)(2,1)}) custom-call(s32[5]{0:T(128)} %pad_add_fusion.meta, bf16[1536,1536]{1,0:T(8,128)(2,1)} %get-tuple-element.50.q_ref.k_ref.v_ref, bf16[1536,1536]{1,0:T(8,128)(2,1)} %get-tuple-element.50.q_ref.k_ref.v_ref, ...), custom_call_target="tpu_custom_call" | custom-call | flops 36238786560 | bytes 12582912 | tf_op jit(solution)/shard_map/pallas_call | solution.py:212
  238.2 9.8 %shard_map.226 = bf16[4,256,1536]{2,1,0:T(8,128)(2,1)} custom-call(s32[4]{0:T(128)} %iota.19.quarters, bf16[1024,1536]{1,0:T(8,128)(2,1)} %get-tuple-element.78.normed_t, bf16[1536,512]{1,0:T(8,128)(2,1)} %get-tuple-element.71.dq, bf16[1536,512]{1,0:T(8,128)(2,1)} %get-tuple-element.72.dk, bf16[1536,512]{1,0:T(8,128)(2,1)} %get-tuple-element.73.dv), custom_call_target="tpu_custom_call" | custom-call | flops 4831838208 | bytes 12582912 | tf_op jit(solution)/shard_map/pallas_call | solution.py:501
  248.2 19.7 %shard_map.224 = (f32[768,1024]{1,0:T(8,128)}, bf16[768,1024]{1,0:T(8,128)(2,1)}) custom-call(bf16[1536,512]{1,0:T(8,128)(2,1)} %get-tuple-element.71.dq, bf16[1536,512]{1,0:T(8,128)(2,1)} %get-tuple-element.72.dk, bf16[1536,512]{1,0:T(8,128)(2,1)} %get-tuple-element.73.dv, bf16[1024,512]{1,0:T(8,128)(2,1)} %wq.5, bf16[1024,512]{1,0:T(8,128)(2,1)} %wk.5, ...), custom_call_target="tpu_custom_call" | custom-call | flops 4831838208 | bytes 18874368 | tf_op jit(solution)/shard_map/pallas_call | solution.py:534
  268.1 4.0 fusion
  272.1 46.3 %psum.55 = f32[1024]{0:T(1024)} all-reduce(f32[1024]{0:T(1024)S(1)} %bitcast.60), channel_id=1, replica_groups=mesh['dp'=16,'mp'=2] {'dp'}, use_global_device_ids=true, to_apply=%region_6.7 | all-reduce | flops 1024 | bytes 8192 | tf_op jit(solution)/shard_map/psum | solution.py:651
  318.3 6.2 shard_map.225
  324.5 41.4 %psum.54 = f32[1024]{0:T(1024)} all-reduce(f32[1024]{0:T(1024)} %bitcast.61), channel_id=1, replica_groups=mesh['dp'=16,'mp'=2] {'dp','mp'}, use_global_device_ids=true, to_apply=%region_5.6 | all-reduce | flops 1024 | bytes 8192 | tf_op jit(solution)/shard_map/psum | solution.py:650
  365.9 257.0 %all-reduce.3.cloned.1.call-done = (bf16[4,256,1536]{2,1,0:T(8,128)(2,1)}, bf16[512,1024]{1,0:T(8,128)(2,1)}, bf16[4,256,1536]{2,1,0:T(8,128)(2,1)}, bf16[4,256,1536]{2,1,0:T(8,128)(2,1)}, bf16[4,256,1152]{2,1,0:T(8,128)(2,1)}) async-done(((bf16[4,256,1536]{2,1,0:T(8,128)(2,1)}, bf16[512,1024]{1,0:T(8,128)(2,1)}, bf16[4,256,1536]{2,1,0:T(8,128)(2,1)}, bf16[4,256,1536]{2,1,0:T(8,128)(2,1)}, ...) | async-done | bytes 12845072 | tf_op jit(solution)/shard_map/psum | solution.py:649
  622.9 3.2 fusion.4
  628.2 3.6 fusion.5
  631.8 1.3 convert_element_type.114
  633.2 2.0 copy.38
  635.2 1.8 convert_element_type.116
  637.0 3.1 fusion.10
  640.1 2.3 copy.35
  642.4 2.7 convert_element_type.108
  645.1 3.7 copy.36
  648.8 3.1 convert_element_type.110
  651.9 2.1 fusion.6
  654.0 1.7 bitcast_convert_fusion
  655.7 1.7 bitcast_convert_fusion.1
  657.4 1.7 bitcast_convert_fusion.2
  659.1 1.6 convert_element_type.101
  660.6 3.3 maximum_convert_fusion.2
  663.9 2.9 maximum_convert_fusion.1
  666.9 2.9 maximum_convert_fusion
  (56 shorter events, 12.5 us)
Async XLA Ops:
  7.2 615.8 %all-reduce.3.cloned.1.call-start = ((), (), s32[]{:S(2)}) async-start(), calls=%async_computation | async-start | bytes 25690112 | tf_op jit(solution)/shard_map/psum | solution.py:649
  7.2 13.3 %collective-permute-start = (bf16[768,1024]{1,0:T(8,128)(2,1)}, bf16[768,1024]{1,0:T(8,128)(2,1)S(1)}, u32[]{:S(2)}, u32[]{:S(2)}) collective-permute-start(bf16[768,1024]{1,0:T(8,128)(2,1)} %bitcast.37), channel_id=1, source_target_pairs={{0,1},{1,0},{2,3},{3,2},{4,5},{5,4},{6,7},{7,6},{8,9},{9,8},{10,11... | collective-permute-start | bytes 4718600 | tf_op jit(solution)/shard_map/ppermute | solution.py:580
  20.5 1.1 copy-start
  55.6 11.2 %copy-start.10 = (bf16[1408,1024]{1,0:T(8,128)(2,1)S(1)}, bf16[1408,1024]{1,0:T(8,128)(2,1)}, u32[]{:S(2)}) copy-start(bf16[1408,1024]{1,0:T(8,128)(2,1)} %refs_11_.1) | copy-start | bytes 8650756
  62.1 12.8 %collective-permute-start.1 = (bf16[1536,1024]{1,0:T(8,128)(2,1)}, bf16[1536,1024]{1,0:T(8,128)(2,1)S(1)}, u32[]{:S(2)}, u32[]{:S(2)}) collective-permute-start(bf16[1536,1024]{1,0:T(8,128)(2,1)} %shard_map.215.mine), channel_id=1, source_target_pairs={{0,1},{1,0},{2,3},{3,2},{4,5},{5,4},{6,7},{7,6},{8,9},{9,8},{10,11... | collective-permute-start | bytes 9437192 | tf_op jit(solution)/shard_map/ppermute | solution.py:580
  62.2 10.5 %collective-permute-start.2 = (bf16[768,1024]{1,0:T(8,128)(2,1)}, bf16[768,1024]{1,0:T(8,128)(2,1)S(1)}, u32[]{:S(2)}, u32[]{:S(2)}) collective-permute-start(bf16[768,1024]{1,0:T(8,128)(2,1)} %bitcast.53), channel_id=1, source_target_pairs={{0,1},{1,0},{2,3},{3,2},{4,5},{5,4},{6,7},{7,6},{8,9},{9,8},{10,11... | collective-permute-start | bytes 4718600 | tf_op jit(solution)/shard_map/ppermute | solution.py:580
  66.9 2.5 copy-start.11
  66.9 3.7 copy-start.12
  70.6 2.3 copy-start.13
  74.9 1.7 copy-start.8
  162.2 5.9 collective-permute-start.4
  168.1 1.7 copy-start.9
  248.0 20.1 %copy-start.7 = (f32[768,1024]{1,0:T(8,128)S(1)}, f32[768,1024]{1,0:T(8,128)}, u32[]{:S(2)}) copy-start(f32[768,1024]{1,0:T(8,128)} %get-tuple-element.64) | copy-start | bytes 9437188
  248.0 20.1 %collective-permute-start.3 = (bf16[768,1024]{1,0:T(8,128)(2,1)}, bf16[768,1024]{1,0:T(8,128)(2,1)S(1)}, u32[]{:S(2)}, u32[]{:S(2)}) collective-permute-start(bf16[768,1024]{1,0:T(8,128)(2,1)} %get-tuple-element.65), channel_id=1, source_target_pairs={{0,1},{1,0},{2,3},{3,2},{4,5},{5,4},{6,7},{7,6},{8,9},{9,8},{10,11... | collective-permute-start | bytes 4718600 | tf_op jit(solution)/shard_map/ppermute | solution.py:580
  267.8 50.5 %collective-permute-start.5 = (bf16[768,1024]{1,0:T(8,128)(2,1)}, bf16[768,1024]{1,0:T(8,128)(2,1)}, u32[]{:S(2)}, u32[]{:S(2)}) collective-permute-start(bf16[768,1024]{1,0:T(8,128)(2,1)} %get-tuple-element.75), channel_id=1, source_target_pairs={{0,1},{1,0},{2,3},{3,2},{4,5},{5,4},{6,7},{7,6},{8,9},{9,8},{10,11... | collective-permute-start | bytes 4718600 | tf_op jit(solution)/shard_map/ppermute | solution.py:580
  268.1 4.0 copy-start.15
  655.7 3.4 copy-start.14
  657.4 3.3 copy-start.6
  660.6 3.3 copy-start.1
  660.6 3.3 copy-start.3
  660.6 3.3 copy-start.5
  663.9 2.9 copy-start.2
  663.9 2.9 copy-start.4
Sparse Core Ops, SparseCore 0:
  248.1 374.8 all-reduce.2
